TPU v7x, 32 devices: a whole 2x2x4 slice. The times are simulated.
32 devices in a mesh: win: 2 (over y), chan: 16 (over z, x, core).
Axes of the slice: x: 2, y: 2, z: 4, core: 2. Of those that a mesh axis runs over, the one named last changes fastest.
Arguments:
- strain_raw: bfloat16 [256, 4352], P('chan', 'win'), may hold values from -6 to 6
- fir_taps: bfloat16 [128], replicated, may hold values from -0.5 to 0.5
- live_mask: int32 [256], P('chan'), may hold values 0 or 1
- window_start: int32 [8], P('win'), may hold values from 0 to 132
Outputs:
- stack: float32 [128, 101, 256], P('chan', None, 'win')
All inputs are finite; a program needn't handle non-finite values. No bound on the sum of `live_mask` on one device may be relied on, other than what follows from the above.
Results may differ from a plain program's by a relative error of at most 0.0018.
Values may be sent and summed in bfloat16 or wider, within the bound.
A program may use at most 128 MiB of HBM per device.

v0:
```python
import math

import jax
import jax.numpy as jnp
from jax import lax
from jax.sharding import PartitionSpec as P

NS = 1024
DECIM = 4
TAPS = 128
HALF = 32
LAGS = 101
STRIDE = 2


EPSILON = 1e-06


def spread(value, axis, source):
    kept = jnp.where(lax.axis_index(axis) == source, value, 0).astype(value.dtype)
    return lax.psum(kept, axis)


def dft_tables(first_bin, bin_count, samples):
    freq_at = first_bin + lax.broadcasted_iota(jnp.int32, (bin_count, samples), 0)
    time_at = lax.broadcasted_iota(jnp.int32, (bin_count, samples), 1)
    phase = freq_at * time_at % samples
    angle = phase.astype(jnp.float32) * (2.0 * math.pi / samples)
    return (jnp.cos(angle), jnp.sin(angle))


def decimate(window, fir_taps, samples, factor):
    tap_count = fir_taps.shape[0]
    block_len = 128
    reach_len = block_len * factor + tap_count - factor
    padded_taps = jnp.concatenate(
        [fir_taps, jnp.zeros((reach_len + factor - tap_count,), fir_taps.dtype)]
    )
    band_rows = jnp.tile(padded_taps, block_len)[: block_len * reach_len].reshape(
        block_len, reach_len
    )
    frames = jnp.stack(
        [
            window[:, part * block_len * factor : part * block_len * factor + reach_len]
            for part in range(samples // block_len)
        ],
        axis=1,
    )
    output = jnp.einsum("cbt,mt->cbm", frames, band_rows, preferred_element_type=jnp.float32)
    return output.reshape(window.shape[0], samples)


def whiten_rows(decimated, live_rows, samples, half_width):
    bin_block = 512
    contract = (((1,), (1,)), ((), ()))
    reals = []
    imags = []
    for first_bin in range(0, samples, bin_block):
        cosine, sine = dft_tables(first_bin, bin_block, samples)
        reals.append(
            lax.dot_general(
                decimated,
                cosine,
                contract,
                precision=lax.Precision.HIGHEST,
                preferred_element_type=jnp.float32,
            )
        )
        imags.append(
            -lax.dot_general(
                decimated,
                sine,
                contract,
                precision=lax.Precision.HIGHEST,
                preferred_element_type=jnp.float32,
            )
        )
    real_part = jnp.concatenate(reals, axis=1)
    imag_part = jnp.concatenate(imags, axis=1)
    amplitude = jnp.sqrt(real_part * real_part + imag_part * imag_part)
    padded = jnp.concatenate(
        [amplitude[:, samples - half_width :], amplitude, amplitude[:, :half_width]], axis=1
    )
    smooth = lax.reduce_window(
        padded, jnp.array(0, jnp.float32), lax.add, (1, 2 * half_width + 1), (1, 1), "VALID"
    ) / (2 * half_width + 1)
    scale = 1.0 / (smooth + EPSILON)
    white_real = real_part * scale
    white_imag = imag_part * scale
    series = jnp.zeros(decimated.shape, jnp.float32)
    for first_bin in range(0, samples, bin_block):
        cosine, sine = dft_tables(first_bin, bin_block, samples)
        series = series + jnp.dot(
            white_real[:, first_bin : first_bin + bin_block],
            cosine,
            precision=lax.Precision.HIGHEST,
            preferred_element_type=jnp.float32,
        )
        series = series - jnp.dot(
            white_imag[:, first_bin : first_bin + bin_block],
            sine,
            precision=lax.Precision.HIGHEST,
            preferred_element_type=jnp.float32,
        )
    series = series * (1.0 / math.sqrt(samples)) * live_rows
    return series.astype(jnp.bfloat16)


def build_lagged(series, lag_count):
    half_lag = lag_count // 2
    samples = series.shape[2]
    extended = jnp.concatenate(
        [series[:, :, samples - half_lag :], series, series[:, :, :half_lag]], axis=2
    )
    shifted = jnp.stack(
        [
            extended[:, :, 2 * half_lag - lag_at : 2 * half_lag - lag_at + samples]
            for lag_at in range(lag_count)
        ],
        axis=0,
    )
    return shifted.reshape(lag_count * series.shape[0], series.shape[1] * samples)


def block_terms(series, sources, windows):
    contract = (((1,), (1,)), ((), ()))
    groups = lax.axis_size("win")
    lagged = build_lagged(series, LAGS)
    scale = 1.0 / (math.sqrt(NS) * math.sqrt(windows * groups))
    return lax.dot_general(sources, lagged, contract, preferred_element_type=jnp.float32) * scale


def arrange_terms(arrived, blocks_total, channels):
    group_rows = arrived.shape[1] // (LAGS * channels)
    arranged = arrived.reshape(blocks_total, group_rows, LAGS, channels).transpose(1, 2, 0, 3)
    return arranged.reshape(group_rows, LAGS, blocks_total * channels)


def local(strain_raw, fir_taps, live_mask, window_start):
    channels = strain_raw.shape[0]
    windows = window_start.shape[0]
    span_len = (NS - 1) * DECIM + TAPS
    record = lax.all_gather(strain_raw, "win", axis=1, tiled=True)
    pieces = []
    for window_at in range(windows):
        window = lax.dynamic_slice_in_dim(record, window_start[window_at], span_len, 1)
        pieces.append(decimate(window, fir_taps, NS, DECIM))
    decimated = jnp.stack(pieces, axis=1).reshape(channels * windows, NS)
    live_rows = jnp.repeat(live_mask.astype(jnp.float32), windows)[:, None]
    series = whiten_rows(decimated, live_rows, NS, HALF).reshape(channels, windows, NS)
    blocks_total = lax.axis_size("chan")
    owner_total = lax.axis_size("chan") // STRIDE

    def take_panel(panel_at, held):
        piece = spread(series, "chan", panel_at * STRIDE)
        return lax.dynamic_update_index_in_dim(held, piece, panel_at, 0)

    panels = lax.fori_loop(
        0, owner_total, take_panel, jnp.zeros((owner_total, channels, windows, NS), jnp.bfloat16)
    )
    sources = panels.reshape(owner_total * channels, windows * NS)
    terms = block_terms(series, sources, windows)
    outgoing = terms.reshape(blocks_total, terms.shape[0] // blocks_total * LAGS * channels)
    arrived = lax.all_to_all(outgoing, "chan", split_axis=0, concat_axis=0, tiled=True)
    return lax.psum_scatter(
        arrange_terms(arrived, blocks_total, channels), "win", scatter_dimension=2, tiled=True
    )


def solution(mesh):
    in_specs = (P("chan", "win"), P(), P("chan"), P("win"))
    out_specs = P("chan", None, "win")
    return jax.shard_map(local, mesh=mesh, in_specs=in_specs, out_specs=out_specs, check_vma=False)
```

profile of v0, /device:TPU:0, one launch (start us, length us, event | category | flops | bytes accessed | tf_op | source)
XLA Modules:
  0.0 982.2 jit_solution(5683568236668287702)
XLA Ops:
  7.4 1.5 fusion.267
  16.4 6.2 all_gather.3
  22.7 0.7 concatenate.120
  23.5 0.4 reshape.40
  26.1 0.6 stack.422
  27.2 9.8 convolution_negate_fusion
  37.0 9.7 fusion.25
  46.8 10.0 %convolution_negate_fusion.1 = f32[64,512]{1,0:T(8,128)S(1)} fusion(f32[64,1024]{1,0:T(8,128)S(1)} %reshape.34), kind=kOutput, calls=%fused_computation.125 | convolution fusion | flops 410025984 | bytes 393216 | tf_op jit(solution)/shard_map/dot_general | solution.py:70
  56.7 19.9 %fusion.18 = f32[64,512]{1,0:T(8,128)S(1)} fusion(f32[64,1024]{1,0:T(8,128)S(1)} %reshape.34), kind=kOutput, calls=%fused_computation.129 | convolution fusion | flops 409993216 | bytes 393216 | tf_op jit(solution)/shard_map/dot_general | solution.py:61
  77.0 9.2 reduce_window.7
  86.3 9.5 fusion.16
  95.7 9.9 %convolution_subtract_fusion.1 = f32[64,1024]{1,0:T(8,128)S(1)} fusion(f32[64,1024]{1,0:T(8,128)S(1)} %fusion.16, f32[64,1024]{1,0:T(8,128)S(1)} %get-tuple-element.100), kind=kOutput, calls=%fused_computation.122 | convolution fusion | flops 410058752 | bytes 655360 | tf_op jit(solution)/shard_map/dot_general | solution.py:99
  105.6 9.1 convolution_add_fusion
  114.9 9.3 fusion.13
  141.5 8.9 copy.145
  150.4 753.5 %while.15 = (s32[]{:T(128)}, bf16[8,16,4,1024]{3,2,1,0:T(4,128)(2,1)S(1)}, bf16[16,4,1024]{2,1,0:T(4,128)(2,1)S(1)}, s32[]{:T(128)}, u32[]{:T(128)}, /*index=5*/s32[]{:T(128)}) while((s32[]{:T(128)}, bf16[8,16,4,1024]{3,2,1,0:T(4,128)(2,1)S(1)}, bf16[16,4,1024]{2,1,0:T(4,128)(2,1)S(1)}, s32[]{:T(128)}, u32[]{:T(128)}, ...), condition=%wide.region_3.4_spmd, body=%wide.region_1.3_spmd.sunk | while | flops 131078 | bytes 1310883 | solution.py:158
  150.4 0.7 select_bitcast_fusion.2
  151.2 92.7 %all-reduce.3.cloned.1.call-done = bf16[1,16,4,1024]{3,2,1,0:T(4,128)(2,1)} async-done(((bf16[1,16,4,1024]{3,2,1,0:T(4,128)(2,1)}), bf16[1,16,4,1024]{3,2,1,0:T(4,128)(2,1)}) %all-reduce.3.cloned.1.call-update) | async-done | bytes 131088 | tf_op jit(solution)/shard_map/while/body/eval_jaxpr/psum | solution.py:21
  243.8 1.0 constant_dynamic-update-slice_fusion.127
  244.9 0.7 select_bitcast_fusion.2
  245.6 92.5 %all-reduce.3.cloned.1.call-done = bf16[1,16,4,1024]{3,2,1,0:T(4,128)(2,1)} async-done(((bf16[1,16,4,1024]{3,2,1,0:T(4,128)(2,1)}), bf16[1,16,4,1024]{3,2,1,0:T(4,128)(2,1)}) %all-reduce.3.cloned.1.call-update) | async-done | bytes 131088 | tf_op jit(solution)/shard_map/while/body/eval_jaxpr/psum | solution.py:21
  338.1 1.0 constant_dynamic-update-slice_fusion.127
  339.2 0.7 select_bitcast_fusion.2
  339.9 92.5 %all-reduce.3.cloned.1.call-done = bf16[1,16,4,1024]{3,2,1,0:T(4,128)(2,1)} async-done(((bf16[1,16,4,1024]{3,2,1,0:T(4,128)(2,1)}), bf16[1,16,4,1024]{3,2,1,0:T(4,128)(2,1)}) %all-reduce.3.cloned.1.call-update) | async-done | bytes 131088 | tf_op jit(solution)/shard_map/while/body/eval_jaxpr/psum | solution.py:21
  432.4 1.0 constant_dynamic-update-slice_fusion.127
  433.4 0.7 select_bitcast_fusion.2
  434.2 92.2 %all-reduce.3.cloned.1.call-done = bf16[1,16,4,1024]{3,2,1,0:T(4,128)(2,1)} async-done(((bf16[1,16,4,1024]{3,2,1,0:T(4,128)(2,1)}), bf16[1,16,4,1024]{3,2,1,0:T(4,128)(2,1)}) %all-reduce.3.cloned.1.call-update) | async-done | bytes 131088 | tf_op jit(solution)/shard_map/while/body/eval_jaxpr/psum | solution.py:21
  526.4 1.0 constant_dynamic-update-slice_fusion.127
  527.4 0.7 select_bitcast_fusion.2
  528.2 92.2 %all-reduce.3.cloned.1.call-done = bf16[1,16,4,1024]{3,2,1,0:T(4,128)(2,1)} async-done(((bf16[1,16,4,1024]{3,2,1,0:T(4,128)(2,1)}), bf16[1,16,4,1024]{3,2,1,0:T(4,128)(2,1)}) %all-reduce.3.cloned.1.call-update) | async-done | bytes 131088 | tf_op jit(solution)/shard_map/while/body/eval_jaxpr/psum | solution.py:21
  620.4 1.0 constant_dynamic-update-slice_fusion.127
  621.4 0.7 select_bitcast_fusion.2
  622.1 92.2 %all-reduce.3.cloned.1.call-done = bf16[1,16,4,1024]{3,2,1,0:T(4,128)(2,1)} async-done(((bf16[1,16,4,1024]{3,2,1,0:T(4,128)(2,1)}), bf16[1,16,4,1024]{3,2,1,0:T(4,128)(2,1)}) %all-reduce.3.cloned.1.call-update) | async-done | bytes 131088 | tf_op jit(solution)/shard_map/while/body/eval_jaxpr/psum | solution.py:21
  714.4 1.0 constant_dynamic-update-slice_fusion.127
  715.4 0.7 select_bitcast_fusion.2
  716.1 92.5 %all-reduce.3.cloned.1.call-done = bf16[1,16,4,1024]{3,2,1,0:T(4,128)(2,1)} async-done(((bf16[1,16,4,1024]{3,2,1,0:T(4,128)(2,1)}), bf16[1,16,4,1024]{3,2,1,0:T(4,128)(2,1)}) %all-reduce.3.cloned.1.call-update) | async-done | bytes 131088 | tf_op jit(solution)/shard_map/while/body/eval_jaxpr/psum | solution.py:21
  808.6 1.0 constant_dynamic-update-slice_fusion.127
  809.7 0.7 select_bitcast_fusion.2
  810.4 92.5 %all-reduce.3.cloned.1.call-done = bf16[1,16,4,1024]{3,2,1,0:T(4,128)(2,1)} async-done(((bf16[1,16,4,1024]{3,2,1,0:T(4,128)(2,1)}), bf16[1,16,4,1024]{3,2,1,0:T(4,128)(2,1)}) %all-reduce.3.cloned.1.call-update) | async-done | bytes 131088 | tf_op jit(solution)/shard_map/while/body/eval_jaxpr/psum | solution.py:21
  902.9 1.0 constant_dynamic-update-slice_fusion.127
  904.3 6.9 convolution_multiply_fusion
  911.5 1.3 all_to_all.8
  912.9 27.1 %all_to_all.10 = f32[16,1,12928]{2,1,0:T(1,128)S(1)} all-to-all(f32[16,1,12928]{2,1,0:T(1,128)S(1)} %all_to_all.8), channel_id=1, replica_groups=mesh['win'=2,'chan'=16] {'chan'}, dimensions={0} | all-to-all | bytes 1654784 | tf_op jit(solution)/shard_map/all_to_all | solution.py:164
  940.0 2.0 reduce
  942.0 5.2 reshape.38
  947.1 5.5 copy.142
  952.6 19.7 %reduce-scatter.2.cloned.1.call-done = f32[8,101,128]{1,2,0:T(8,128)} async-done(((f32[8,101,256]{1,2,0:T(8,128)}), f32[8,101,128]{1,2,0:T(8,128)}) %reduce-scatter.2.cloned.1.call-update) | async-done | bytes 413712 | tf_op jit(solution)/shard_map/reduce_scatter | solution.py:165
  972.4 2.0 copy.143
  (169 shorter events, 21.7 us)
Async XLA Ops:
  86.2 28.4 %copy-start = (s32[16]{0:T(128)S(1)}, s32[16]{0:T(128)}, u32[]{:S(2)}) copy-start(s32[16]{0:T(128)} %param.8) | copy-start | bytes 196
  150.4 93.4 %all-reduce.3.cloned.1.call-start = ((), (), s32[]{:S(2)}) async-start(), calls=%async_computation.3 | async-start | bytes 262144 | tf_op jit(solution)/shard_map/while/body/eval_jaxpr/psum | solution.py:21
  244.8 93.3 %all-reduce.3.cloned.1.call-start = ((), (), s32[]{:S(2)}) async-start(), calls=%async_computation.3 | async-start | bytes 262144 | tf_op jit(solution)/shard_map/while/body/eval_jaxpr/psum | solution.py:21
  339.1 93.3 %all-reduce.3.cloned.1.call-start = ((), (), s32[]{:S(2)}) async-start(), calls=%async_computation.3 | async-start | bytes 262144 | tf_op jit(solution)/shard_map/while/body/eval_jaxpr/psum | solution.py:21
  433.4 93.0 %all-reduce.3.cloned.1.call-start = ((), (), s32[]{:S(2)}) async-start(), calls=%async_computation.3 | async-start | bytes 262144 | tf_op jit(solution)/shard_map/while/body/eval_jaxpr/psum | solution.py:21
  527.4 93.0 %all-reduce.3.cloned.1.call-start = ((), (), s32[]{:S(2)}) async-start(), calls=%async_computation.3 | async-start | bytes 262144 | tf_op jit(solution)/shard_map/while/body/eval_jaxpr/psum | solution.py:21
  621.3 93.0 %all-reduce.3.cloned.1.call-start = ((), (), s32[]{:S(2)}) async-start(), calls=%async_computation.3 | async-start | bytes 262144 | tf_op jit(solution)/shard_map/while/body/eval_jaxpr/psum | solution.py:21
  715.3 93.3 %all-reduce.3.cloned.1.call-start = ((), (), s32[]{:S(2)}) async-start(), calls=%async_computation.3 | async-start | bytes 262144 | tf_op jit(solution)/shard_map/while/body/eval_jaxpr/psum | solution.py:21
  809.6 93.3 %all-reduce.3.cloned.1.call-start = ((), (), s32[]{:S(2)}) async-start(), calls=%async_computation.3 | async-start | bytes 262144 | tf_op jit(solution)/shard_map/while/body/eval_jaxpr/psum | solution.py:21
  903.9 68.4 %reduce-scatter.2.cloned.1.call-start = ((), (), s32[]{:S(2)}) async-start(), calls=%async_computation.2 | async-start | bytes 1572864 | tf_op jit(solution)/shard_map/reduce_scatter | solution.py:165
Sparse Core Ops, SparseCore 0:
  155.1 88.6 all-reduce.2
  249.5 88.5 all-reduce.2
  343.8 88.5 all-reduce.2
  437.8 88.5 all-reduce.2
  531.7 88.5 all-reduce.2
  625.7 88.5 all-reduce.2
  720.0 88.5 all-reduce.2
  814.3 88.5 all-reduce.2
Sparse Core Ops, SparseCore 1:
  952.7 19.6 reduce-scatter.1
where the time goes:
time: 992 us; the launch traced here: 982 us
  waiting for transfers between devices  759 us (77%)
  matrix products  94.8 us (10%)
  local copies, waits for them, and re-layouts  36.9 us (4%)
  other arithmetic  34 us (3%)
  blocking collectives  33.3 us (3%)
  between operations  23.3 us (2%)
    psum x8, waiting for transfers between devices, spread(): return lax.psum(kept, axis)  739 us
    dot_general x2, matrix products, whiten_rows(): lax.dot_general(decimated, cosine, contract, precision=lax.Precision.HIGH...  29.6 us
    all_to_all x1, blocking collectives, local(): lax.all_to_all(outgoing, 'chan', split_axis=0, concat_axis=0, tiled=True)  27.1 us
  transfers between devices with their start and end apart: 9, of which 9 were waited for; matrix products, arithmetic and copies ran while one was open for 0% of the time, Pallas kernels for 0%

commit v1 on v0

v1 whole, which is shorter than its diff:
```python
import math

import jax
import jax.numpy as jnp
import ml_dtypes
import numpy as np
from jax import lax
from jax.experimental import pallas as pl
from jax.experimental.pallas import tpu as pltpu
from jax.sharding import PartitionSpec as P

NS = 1024
DECIM = 4
TAPS = 128
HALF = 32
LAGS = 101
STRIDE = 2
EPSILON = 1e-06

FOLD = NS // 2
BLOCK = 128
REACH = BLOCK * DECIM + TAPS
LAG_ROWS = 112
VMEM_LIMIT = 48 * 1024 * 1024


def split_table(table):
    high = table.astype(ml_dtypes.bfloat16)
    low = (table - high.astype(np.float64)).astype(ml_dtypes.bfloat16)
    return high, low


def build_tables():
    time_at = np.arange(FOLD)
    forward = []
    inverse = []
    for parity in range(2):
        bins = 2 * np.arange(NS // 4) + parity
        angle = 2.0 * np.pi * ((time_at[:, None] * bins[None, :]) % NS) / NS
        cosine = np.cos(angle)
        sine = -np.sin(angle)
        weight = np.full((2 * bins.size,), 2.0 / math.sqrt(NS))
        if parity == 0:
            sine[:, 0] = np.cos(np.pi * time_at)
            weight[0] = 1.0 / math.sqrt(NS)
            weight[bins.size] = 1.0 / math.sqrt(NS)
        table = np.concatenate([cosine, sine], axis=1)
        forward.append(table)
        inverse.append((table * weight[None, :]).T)
    order = np.concatenate([np.arange(0, FOLD, 2), np.arange(1, FOLD, 2), [FOLD]])
    place = np.zeros((FOLD + 1,), np.int64)
    place[order] = np.arange(FOLD + 1)
    counts = np.zeros((FOLD + 1, FOLD + 1))
    for column, bin_at in enumerate(order):
        for offset in range(-HALF, HALF + 1):
            seen = (bin_at + offset) % NS
            counts[place[min(seen, NS - seen)], column] += 1.0
    mean_table = counts[:FOLD, :FOLD].astype(ml_dtypes.bfloat16)
    edge = np.zeros((8, FOLD), np.float32)
    edge[0] = counts[FOLD, :FOLD]
    edge[1] = counts[:FOLD, FOLD]
    forward_high, forward_low = split_table(np.stack(forward))
    inverse_high, inverse_low = split_table(np.stack(inverse))
    return forward_high, forward_low, inverse_high, inverse_low, mean_table, edge


def dot(left, right):
    return jnp.dot(left, right, preferred_element_type=jnp.float32)


def split_dot(value, high, low):
    rows = value.shape[0]
    value_high = value.astype(jnp.bfloat16)
    value_low = (value - value_high.astype(jnp.float32)).astype(jnp.bfloat16)
    both = dot(jnp.concatenate([value_high, value_low], axis=0), high)
    return both[:rows] + both[rows:] + dot(value_high, low)


def whiten_kernel(windows, starts, record, band, forward_high, forward_low, inverse_high, inverse_low,
                  mean_table, edge, live, out):
    channels, length = record.shape
    wide = record[...].astype(jnp.float32)
    pieces = []
    for window_at in range(windows):
        start = starts[window_at]
        rolled = pltpu.roll(wide, lax.rem(length - start, length), 1).astype(jnp.bfloat16)
        parts = [
            dot(rolled[:, at * BLOCK * DECIM : at * BLOCK * DECIM + REACH], band[...])
            for at in range(NS // BLOCK)
        ]
        pieces.append(jnp.concatenate(parts, axis=1))
    decimated = jnp.concatenate(pieces, axis=0)
    first, second = decimated[:, :FOLD], decimated[:, FOLD:]
    even = split_dot(first + second, forward_high[0], forward_low[0])
    odd = split_dot(first - second, forward_high[1], forward_low[1])
    quarter = NS // 4
    real_part = jnp.concatenate([even[:, :quarter], odd[:, :quarter]], axis=1)
    imag_part = jnp.concatenate([even[:, quarter:], odd[:, quarter:]], axis=1)
    at_zero = lax.broadcasted_iota(jnp.int32, real_part.shape, 1) == 0
    amplitude = jnp.sqrt(real_part * real_part + jnp.where(at_zero, 0.0, imag_part * imag_part))
    top = jnp.abs(imag_part[:, 0:1])
    amp_high = amplitude.astype(jnp.bfloat16)
    amp_low = (amplitude - amp_high.astype(jnp.float32)).astype(jnp.bfloat16)
    summed = dot(amp_high, mean_table[...]) + dot(amp_low, mean_table[...]) + top * edge[0:1, :]
    summed_top = jnp.sum(amplitude * edge[1:2, :], axis=1, keepdims=True) + top
    width = 2 * HALF + 1
    scale = 1.0 / (summed * (1.0 / width) + EPSILON)
    scale_top = 1.0 / (summed_top * (1.0 / width) + EPSILON)
    white_real = real_part * scale
    white_imag = imag_part * jnp.where(at_zero, scale_top, scale)
    white_even = jnp.concatenate([white_real[:, :quarter], white_imag[:, :quarter]], axis=1)
    white_odd = jnp.concatenate([white_real[:, quarter:], white_imag[:, quarter:]], axis=1)
    from_even = split_dot(white_even, inverse_high[0], inverse_low[0])
    from_odd = split_dot(white_odd, inverse_high[1], inverse_low[1])
    series = jnp.concatenate([from_even + from_odd, from_even - from_odd], axis=1)
    for window_at in range(windows):
        rows = series[window_at * channels : (window_at + 1) * channels]
        out[window_at] = (rows * live[...]).astype(jnp.bfloat16)


def lag_sums(place, gathered, turned, lagged):
    blocks, windows, channels, _ = gathered.shape
    sources = channels // STRIDE
    chan_at = place[1]
    source_block = chan_at // STRIDE * STRIDE
    source_part = lax.rem(chan_at, STRIDE)
    total = None
    for window_at in range(windows):
        rows = gathered[source_block, window_at].astype(jnp.float32)
        chosen = jnp.where(source_part == 0, rows[:sources], rows[sources:])
        for row in range(8):
            turned[:, row, :] = pltpu.roll(chosen, (NS - row) % NS, 1)
        for source in range(sources):
            base = turned[source]
            for first in range(0, LAG_ROWS, 16):
                pair = [pltpu.roll(base, (LAGS // 2 - first - 8 * at) % NS, 1) for at in range(2)]
                lagged[source, first : first + 16, :] = jnp.concatenate(pair, axis=0).astype(jnp.bfloat16)
        term = lax.dot_general(
            lagged[...].reshape(sources * LAG_ROWS, NS),
            gathered[:, window_at].reshape(blocks * channels, NS),
            (((1,), (1,)), ((), ())),
            preferred_element_type=jnp.float32,
        )
        total = term if total is None else total + term
    return total


def corr_pair_kernel(scale, place, gathered, own, other, turned, lagged):
    total = lag_sums(place, gathered, turned, lagged) * scale
    half = total.shape[1] // 2
    first, second = total[:, :half], total[:, half:]
    is_first = place[0] == 0
    kept = jnp.where(is_first, first, second)
    sent = jnp.where(is_first, second, first).astype(jnp.bfloat16)
    for source in range(own.shape[0]):
        at = source * LAG_ROWS
        own[source] = kept[at : at + LAGS]
        other[source] = sent[at : at + LAG_ROWS]


def corr_all_kernel(scale, place, gathered, own, turned, lagged):
    total = lag_sums(place, gathered, turned, lagged) * scale
    for source in range(own.shape[0]):
        own[source] = total[source * LAG_ROWS : source * LAG_ROWS + LAGS]


def whole_in_vmem(count):
    return [pl.BlockSpec(memory_space=pltpu.VMEM)] * count


def local(tables, strain_raw, fir_taps, live_mask, window_start):
    channels = strain_raw.shape[0]
    windows = window_start.shape[0]
    groups = lax.axis_size("win")
    blocks = lax.axis_size("chan")
    win_at = lax.axis_index("win")
    chan_at = lax.axis_index("chan")
    record = lax.all_gather(strain_raw, "win", axis=1, tiled=True)
    padded = jnp.concatenate([fir_taps, jnp.zeros((REACH + DECIM - TAPS,), fir_taps.dtype)])
    band = jnp.tile(padded, BLOCK)[: BLOCK * REACH].reshape(BLOCK, REACH).T
    params = pltpu.CompilerParams(vmem_limit_bytes=VMEM_LIMIT)
    smem = pl.BlockSpec(memory_space=pltpu.SMEM)
    series = pl.pallas_call(
        lambda *refs: whiten_kernel(windows, *refs),
        out_shape=jax.ShapeDtypeStruct((windows, channels, NS), jnp.bfloat16),
        in_specs=[smem] + whole_in_vmem(9),
        out_specs=pl.BlockSpec(memory_space=pltpu.VMEM),
        compiler_params=params,
        name="whiten",
    )(window_start, record, band, *tables, live_mask.astype(jnp.float32)[:, None])
    gathered = lax.all_gather(series, "chan", axis=0, tiled=False)
    place = jnp.stack([win_at, chan_at]).astype(jnp.int32)
    scale = 1.0 / (math.sqrt(NS) * math.sqrt(windows * groups))
    sources = channels // STRIDE
    scratch = [
        pltpu.VMEM((sources, 8, NS), jnp.float32),
        pltpu.VMEM((sources, LAG_ROWS, NS), jnp.bfloat16),
    ]
    total = blocks * channels
    if groups == 2:
        own, other = pl.pallas_call(
            lambda *refs: corr_pair_kernel(scale, *refs),
            out_shape=[
                jax.ShapeDtypeStruct((sources, LAGS, total // 2), jnp.float32),
                jax.ShapeDtypeStruct((sources, LAG_ROWS, total // 2), jnp.bfloat16),
            ],
            in_specs=[smem] + whole_in_vmem(1),
            out_specs=whole_in_vmem(2),
            scratch_shapes=scratch,
            compiler_params=params,
            name="correlate",
        )(place, gathered)
        arrived = lax.ppermute(other, "win", [(0, 1), (1, 0)])
        return own + arrived[:, :LAGS].astype(jnp.float32)
    own = pl.pallas_call(
        lambda *refs: corr_all_kernel(scale, *refs),
        out_shape=jax.ShapeDtypeStruct((sources, LAGS, total), jnp.float32),
        in_specs=[smem] + whole_in_vmem(1),
        out_specs=pl.BlockSpec(memory_space=pltpu.VMEM),
        scratch_shapes=scratch,
        compiler_params=params,
        name="correlate",
    )(place, gathered)
    return lax.psum_scatter(own, "win", scatter_dimension=2, tiled=True)


def solution(mesh):
    in_specs = (P("chan", "win"), P(), P("chan"), P("win"))
    out_specs = P("chan", None, "win")

    def run(strain_raw, fir_taps, live_mask, window_start):
        tables = [jnp.asarray(table) for table in build_tables()]
        mapped = jax.shard_map(
            lambda tables, *args: local(tables, *args),
            mesh=mesh,
            in_specs=(P(),) + in_specs,
            out_specs=out_specs,
            check_vma=False,
        )
        return mapped(tables, strain_raw, fir_taps, live_mask, window_start)

    return run
```

time: 992 us -> 88.4 us (0.09)
  waiting for transfers between devices: 759 us -> 49.5 us
  matrix products: 94.8 us -> 0 us
  other arithmetic: 34 us -> 0.89 us
  local copies, waits for them, and re-layouts: 36.9 us -> 8.9 us
  blocking collectives: 33.3 us -> 6.17 us
    psum x8 -> x0, waiting for transfers between devices: 739 us -> none  [spread(): return lax.psum(kept, axis)]
    dot_general x13 -> x0, matrix products: 94.8 us -> none  [the longest x2 29.6 us: whiten_rows(): lax.dot_general(decimated, cosine, contract, precision=lax.Precision.HIGH...]
    all_gather x0 -> x1, waiting for transfers between devices: none -> 43.2 us  [local(): gathered = lax.all_gather(series, 'chan', axis=0, tiled=False)]
    all_to_all x1 -> x0, blocking collectives: 27.1 us -> none  [local(): lax.all_to_all(outgoing, 'chan', split_axis=0, concat_axis=0, tiled=True)]
    reduce_scatter x1 -> x0, waiting for transfers between devices: 19.7 us -> none  [local(): lax.psum_scatter(arrange_terms(arrived, blocks_total, channels), 'win', s...]
    unnamed x99 -> x0, other arithmetic: 16.8 us -> none
  transfers between devices with their start and end apart: 9 -> 2, of which waited for: 9 -> 2; matrix products, arithmetic and copies ran while one was open for 0% -> 0% of each run, Pallas kernels for 0% -> 0%
where the time goes in v1:
time: 88.4 us; the launch traced here: 88 us
  waiting for transfers between devices  49.5 us (56%)
  between operations  13.5 us (15%)
  local copies, waits for them, and re-layouts  8.9 us (10%)
  Pallas kernels  7.57 us (9%)
  blocking collectives  6.17 us (7%)
  starting transfers between devices  1.54 us (2%)
  other arithmetic  0.89 us (1%)
    all_gather x1, waiting for transfers between devices, local(): gathered = lax.all_gather(series, 'chan', axis=0, tiled=False)  43.2 us
    unnamed x16, local copies, waits for them, and re-layouts  6.64 us
    ppermute x1, waiting for transfers between devices, local(): arrived = lax.ppermute(other, 'win', [(0, 1), (1, 0)])  6.29 us
    all_gather x1, blocking collectives, local(): record = lax.all_gather(strain_raw, 'win', axis=1, tiled=True)  6.17 us
    pallas_call x1, Pallas kernels, local(): pl.pallas_call(lambda *refs: corr_pair_kernel(scale, *refs), out_shape=[j...  4.14 us
    pallas_call x1, Pallas kernels, local(): pl.pallas_call(lambda *refs: whiten_kernel(windows, *refs), out_shape=jax...  3.42 us
  transfers between devices with their start and end apart: 2, of which 2 were waited for; matrix products, arithmetic and copies ran while one was open for 0% of the time, Pallas kernels for 0%

profile of v1, /device:TPU:0, one launch (start us, length us, event | category | flops | bytes accessed | tf_op | source)
XLA Modules:
  0.0 88.0 jit_solution(1786625714067002157)
XLA Ops:
  6.5 0.0 copy-start.5
  6.5 0.0 copy-start.1
  6.5 0.0 all-gather.3.cloned.1.call-start
  6.5 0.8 convert_bitcast_fusion
  7.3 0.1 copy.17.refs_9_
  7.4 6.2 %all_gather.9.refs_1_ = bf16[16,4352]{1,0:T(8,128)(2,1)S(1)} all-gather(bf16[16,2176]{1,0:T(8,128)(2,1)} %param.10), channel_id=1, replica_groups=mesh['win'=2,'chan'=16] {'win'}, dimensions={1}, use_global_device_ids=true | all-gather | bytes 208896 | tf_op jit(solution)/shard_map/all_gather | solution.py:178
  13.6 0.7 concatenate.3
  14.3 0.4 tile.10
  14.6 0.1 reshape.4
  14.8 0.2 copy.16
  14.9 0.0 copy-done.5
  15.0 0.0 copy-done.1
  15.0 0.0 copy-start.2
  15.0 1.2 %copy-done.2 = bf16[2,512,512]{2,1,0:T(8,128)(2,1)S(1)} copy-done((bf16[2,512,512]{2,1,0:T(8,128)(2,1)S(1)}, bf16[2,512,512]{2,1,0:T(8,128)(2,1)}, u32[]{:S(2)}) %copy-start.2) | copy-done | bytes 1048600
  16.2 0.0 copy-start.3
  16.2 1.2 %copy-done.3 = bf16[2,512,512]{2,1,0:T(8,128)(2,1)S(1)} copy-done((bf16[2,512,512]{2,1,0:T(8,128)(2,1)S(1)}, bf16[2,512,512]{2,1,0:T(8,128)(2,1)}, u32[]{:S(2)}) %copy-start.3) | copy-done | bytes 1048600
  17.4 0.0 copy-start.4
  17.4 1.2 %copy-done.4 = bf16[2,512,512]{2,1,0:T(8,128)(2,1)S(1)} copy-done((bf16[2,512,512]{2,1,0:T(8,128)(2,1)S(1)}, bf16[2,512,512]{2,1,0:T(8,128)(2,1)}, u32[]{:S(2)}) %copy-start.4) | copy-done | bytes 1048600
  18.6 0.0 copy-start.6
  18.6 0.7 copy-done.6
  19.4 0.0 copy-start.7
  19.4 0.7 copy-done.7
  20.0 3.4 %whiten.1 = bf16[4,16,1024]{2,1,0:T(8,128)(2,1)} custom-call(s32[4]{0:T(128)S(1)} %copy-done.7, bf16[16,4352]{1,0:T(8,128)(2,1)S(1)} %all_gather.9.refs_1_, bf16[640,128]{1,0:T(8,128)(2,1)S(1)} %bitcast.7, bf16[2,512,512]{2,1,0:T(8,128)(2,1)S(1)} %copy-done.4, bf16[2,512,512]{2,1,0:T(8,128)(2,1)S(1)} %copy-done.3, bf16[2,512,512]{2,1,0:T(8,128)(2,1)S(1)} %copy-done.2, ...), custom_call_target="tpu_custom_call" | custom-call | tf_op jit(solution)/shard_map/whiten/pallas_call | solution.py:183
  23.4 0.0 all-gather.3.cloned.1.call-update
  23.5 0.1 pad_add_fusion.refs_0_
  23.5 43.2 %all-gather.3.cloned.1.call-done = bf16[64,16,1024]{2,1,0:T(8,128)(2,1)} async-done(((bf16[4,16,1024]{2,1,0:T(8,128)(2,1)}), bf16[64,16,1024]{2,1,0:T(8,128)(2,1)}) %all-gather.3.cloned.1.call-update) | async-done | bytes 2097168 | tf_op jit(solution)/shard_map/all_gather | solution.py:191
  66.7 0.0 copy-start
  66.7 1.6 %copy-done = bf16[64,16,1024]{2,1,0:T(8,128)(2,1)S(1)} copy-done((bf16[64,16,1024]{2,1,0:T(8,128)(2,1)S(1)}, bf16[64,16,1024]{2,1,0:T(8,128)(2,1)}, u32[]{:S(2)}) %copy-start) | copy-done | bytes 2097176
  68.3 4.1 %correlate.1 = (f32[8,101,128]{2,1,0:T(8,128)S(1)}, bf16[8,112,128]{2,1,0:T(8,128)(2,1)S(1)}) custom-call(s32[2]{0:T(128)S(1)} %pad_add_fusion.refs_0_, bf16[16,4,16,1024]{3,2,1,0:T(8,128)(2,1)S(1)} %bitcast.6), custom_call_target="tpu_custom_call" | custom-call | tf_op jit(solution)/shard_map/correlate/pallas_call | solution.py:201
  72.5 1.5 %collective-permute-start = (bf16[8,112,128]{2,1,0:T(8,128)(2,1)S(1)}, bf16[8,112,128]{2,1,0:T(8,128)(2,1)S(1)}, u32[]{:S(2)}, u32[]{:S(2)}) collective-permute-start(bf16[8,112,128]{2,1,0:T(8,128)(2,1)S(1)} %get-tuple-element.8), channel_id=1, source_target_pairs={{0,16},{16,0},{1,17},{17,1},{2,18},{18,2},{3,19},{19,3},{4,20},{20... | collective-permute-start | bytes 688136 | tf_op jit(solution)/shard_map/ppermute | solution.py:213
  74.0 6.3 %collective-permute-done = bf16[8,112,128]{2,1,0:T(8,128)(2,1)S(1)} collective-permute-done((bf16[8,112,128]{2,1,0:T(8,128)(2,1)S(1)}, bf16[8,112,128]{2,1,0:T(8,128)(2,1)S(1)}, u32[]{:S(2)}, u32[]{:S(2)}) %collective-permute-start) | collective-permute-done | bytes 229408 | tf_op jit(solution)/shard_map/ppermute | solution.py:213
  80.3 0.8 copy.18
  (3 shorter events, 0.1 us)
Async XLA Ops:
  6.5 8.4 %copy-start.5 = (bf16[512,512]{1,0:T(8,128)(2,1)S(1)}, bf16[512,512]{1,0:T(8,128)(2,1)}, u32[]{:S(2)}) copy-start(bf16[512,512]{1,0:T(8,128)(2,1)} %constant.27.clone.refs_7_) | copy-start | bytes 1572868
  6.5 8.4 %copy-start.1 = (bf16[2,512,512]{2,1,0:T(8,128)(2,1)S(1)}, bf16[2,512,512]{2,1,0:T(8,128)(2,1)}, u32[]{:S(2)}) copy-start(bf16[2,512,512]{2,1,0:T(8,128)(2,1)} %constant.26.clone.refs_6_) | copy-start | bytes 3145732
  6.5 60.2 %all-gather.3.cloned.1.call-start = ((), (), s32[]{:S(2)}) async-start(), calls=%async_computation | async-start | bytes 2228224 | tf_op jit(solution)/shard_map/all_gather | solution.py:191
  15.0 1.2 %copy-start.2 = (bf16[2,512,512]{2,1,0:T(8,128)(2,1)S(1)}, bf16[2,512,512]{2,1,0:T(8,128)(2,1)}, u32[]{:S(2)}) copy-start(bf16[2,512,512]{2,1,0:T(8,128)(2,1)} %constant.25.clone.refs_5_) | copy-start | bytes 3145732
  16.2 1.2 %copy-start.3 = (bf16[2,512,512]{2,1,0:T(8,128)(2,1)S(1)}, bf16[2,512,512]{2,1,0:T(8,128)(2,1)}, u32[]{:S(2)}) copy-start(bf16[2,512,512]{2,1,0:T(8,128)(2,1)} %constant.24.clone.refs_4_) | copy-start | bytes 3145732
  17.4 1.2 %copy-start.4 = (bf16[2,512,512]{2,1,0:T(8,128)(2,1)S(1)}, bf16[2,512,512]{2,1,0:T(8,128)(2,1)}, u32[]{:S(2)}) copy-start(bf16[2,512,512]{2,1,0:T(8,128)(2,1)} %constant.23.clone.refs_3_) | copy-start | bytes 3145732
  18.6 0.7 copy-start.6
  19.4 0.7 copy-start.7
  66.7 1.6 %copy-start = (bf16[64,16,1024]{2,1,0:T(8,128)(2,1)S(1)}, bf16[64,16,1024]{2,1,0:T(8,128)(2,1)}, u32[]{:S(2)}) copy-start(bf16[64,16,1024]{2,1,0:T(8,128)(2,1)} %all-gather.3.cloned.1.call-done) | copy-start | bytes 6291460
  72.5 7.8 %collective-permute-start = (bf16[8,112,128]{2,1,0:T(8,128)(2,1)S(1)}, bf16[8,112,128]{2,1,0:T(8,128)(2,1)S(1)}, u32[]{:S(2)}, u32[]{:S(2)}) collective-permute-start(bf16[8,112,128]{2,1,0:T(8,128)(2,1)S(1)} %get-tuple-element.8), channel_id=1, source_target_pairs={{0,16},{16,0},{1,17},{17,1},{2,18},{18,2},{3,19},{19,3},{4,20},{20... | collective-permute-start | bytes 688136 | tf_op jit(solution)/shard_map/ppermute | solution.py:213
Sparse Core Ops, SparseCore 0:
  23.6 43.0 all-gather.2

commit v2 on v1

--- a/solution.py
+++ b/solution.py
@@ -145,17 +145,171 @@
     return total
 
 
-def corr_pair_kernel(scale, place, gathered, own, other, turned, lagged):
-    total = lag_sums(place, gathered, turned, lagged) * scale
-    half = total.shape[1] // 2
-    first, second = total[:, :half], total[:, half:]
-    is_first = place[0] == 0
-    kept = jnp.where(is_first, first, second)
-    sent = jnp.where(is_first, second, first).astype(jnp.bfloat16)
-    for source in range(own.shape[0]):
-        at = source * LAG_ROWS
-        own[source] = kept[at : at + LAGS]
-        other[source] = sent[at : at + LAG_ROWS]
+def gather_corr_kernel(scale, series, out, held, turned, lagged, outgoing, arrived,
+                       sent, landed, swap_sent, swap_landed):
+    blocks, windows, channels, _ = held.shape
+    sources = channels // STRIDE
+    layers = blocks // 4
+    win_at = lax.axis_index("win")
+    me = lax.axis_index("chan")
+    layer, core = me // 4, lax.rem(me, 2)
+    lane = lax.rem(me, 4)
+    beside = layer * 4 + lax.rem(lane + 2, 4)
+    twin = me + 1 - 2 * core
+    twin_lane = lane + 1 - 2 * core
+    other_lane = lax.rem(lane + 2, 4)
+    partner = 1 - win_at
+    above, below = me + 4, me - 4
+    has_above, has_below = layer < layers - 1, layer > 0
+    mesh_id = pl.DeviceIdType.MESH
+
+    barrier = pltpu.get_barrier_semaphore()
+    pl.semaphore_signal(barrier, inc=1, device_id=(win_at, beside), device_id_type=mesh_id)
+    pl.semaphore_signal(barrier, inc=1, device_id=(win_at, twin), device_id_type=mesh_id)
+    pl.semaphore_signal(barrier, inc=1, device_id=(partner, me), device_id_type=mesh_id)
+
+    @pl.when(has_above)
+    def _():
+        pl.semaphore_signal(barrier, inc=1, device_id=(win_at, above), device_id_type=mesh_id)
+
+    @pl.when(has_below)
+    def _():
+        pl.semaphore_signal(barrier, inc=1, device_id=(win_at, below), device_id_type=mesh_id)
+
+    held[me] = series[...]
+    pl.semaphore_wait(barrier, 3 + has_above.astype(jnp.int32) + has_below.astype(jnp.int32))
+
+    def move(way, block, target):
+        return pltpu.make_async_remote_copy(
+            src_ref=held.at[block],
+            dst_ref=held.at[block],
+            send_sem=sent.at[way, block],
+            recv_sem=landed.at[block],
+            device_id=(win_at, target),
+            device_id_type=mesh_id,
+        )
+
+    def up(block):
+        return move(0, block, above)
+
+    def down(block):
+        return move(1, block, below)
+
+    def across(block):
+        return move(2, block, beside)
+
+    def over(block):
+        return move(3, block, twin)
+
+    def await_block(block):
+        move(2, block, beside).wait_recv()
+
+    def when(condition, action):
+        @pl.when(condition)
+        def _():
+            action()
+
+    when(has_above, lambda: up(me).start())
+    when(has_below, lambda: down(me).start())
+    across(me).start()
+    over(me).start()
+
+    await_block(twin)
+    source_block = me // STRIDE * STRIDE
+    source_part = lax.rem(me, STRIDE)
+
+    def build(window_at, carry):
+        rows = held[source_block, window_at].astype(jnp.float32)
+        chosen = jnp.where(source_part == 0, rows[:sources], rows[sources:])
+        for row in range(8):
+            turned[:, row, :] = pltpu.roll(chosen, (NS - row) % NS, 1)
+
+        def build_source(source, carry):
+            base = turned[source]
+            for first in range(0, LAG_ROWS, 16):
+                pair = [pltpu.roll(base, (LAGS // 2 - first - 8 * at) % NS, 1) for at in range(2)]
+                lagged[window_at, source, first : first + 16, :] = jnp.concatenate(pair, axis=0).astype(jnp.bfloat16)
+            return carry
+
+        return lax.fori_loop(0, sources, build_source, carry)
+
+    def pass_lane(distance):
+        for sign in (-1, 1):
+            origin = layer + sign * distance
+            block = me + 4 * sign * distance
+            exists = (origin >= 0) if sign < 0 else (origin < layers)
+            further = has_above if sign < 0 else has_below
+
+            def relay():
+                await_block(block)
+                when(further, lambda: (up if sign < 0 else down)(block).start())
+                across(block).start()
+                over(block).start()
+
+            when(exists, relay)
+
+    def pass_beside(distance):
+        for sign in (-1, 1) if distance else (1,):
+            origin = layer + sign * distance
+            block = origin * 4 + other_lane
+            exists = (origin >= 0) if sign < 0 else (origin < layers)
+
+            def relay():
+                await_block(block)
+                over(block).start()
+
+            when(exists, relay)
+
+    lax.fori_loop(0, windows, build, 0)
+    pass_lane(1)
+    pass_beside(0)
+    for distance in range(2, layers):
+        pass_lane(distance)
+        pass_beside(distance - 1)
+    pass_beside(layers - 1)
+    for at in range(layers):
+        across_twin = at * 4 + lax.rem(twin_lane + 2, 4)
+        await_block(across_twin)
+        mine = at * 4 + twin_lane
+        when(mine != twin, lambda: await_block(mine))
+
+    half_blocks = blocks // 2
+
+    def half_sums(half):
+        total = None
+        for window_at in range(windows):
+            term = lax.dot_general(
+                lagged[window_at].reshape(sources * LAG_ROWS, NS),
+                held[pl.ds(half * half_blocks, half_blocks), window_at].reshape(half_blocks * channels, NS),
+                (((1,), (1,)), ((), ())),
+                preferred_element_type=jnp.float32,
+            )
+            total = term if total is None else total + term
+        return total * scale
+
+    outgoing[...] = half_sums(partner).astype(jnp.bfloat16).reshape(outgoing.shape)
+    swap = pltpu.make_async_remote_copy(
+        src_ref=outgoing,
+        dst_ref=arrived,
+        send_sem=swap_sent,
+        recv_sem=swap_landed,
+        device_id=(partner, me),
+        device_id_type=mesh_id,
+    )
+    swap.start()
+    kept = half_sums(win_at).reshape(outgoing.shape)
+    swap.wait()
+    total = kept + arrived[...].astype(jnp.float32)
+    for source in range(sources):
+        out[source] = total[source, :LAGS]
+
+    for at in range(layers):
+        block = at * 4 + lane
+        when(jnp.logical_and(has_above, at <= layer), lambda: up(block).wait_send())
+        when(jnp.logical_and(has_below, at >= layer), lambda: down(block).wait_send())
+        across(block).wait_send()
+        over(block).wait_send()
+        over(at * 4 + other_lane).wait_send()
 
 
 def corr_all_kernel(scale, place, gathered, own, turned, lagged):
@@ -188,30 +342,37 @@
         compiler_params=params,
         name="whiten",
     )(window_start, record, band, *tables, live_mask.astype(jnp.float32)[:, None])
+    scale = 1.0 / (math.sqrt(NS) * math.sqrt(windows * groups))
+    sources = channels // STRIDE
+    total = blocks * channels
+    if groups == 2 and blocks == 16:
+        return pl.pallas_call(
+            lambda *refs: gather_corr_kernel(scale, *refs),
+            out_shape=jax.ShapeDtypeStruct((sources, LAGS, total // 2), jnp.float32),
+            in_specs=whole_in_vmem(1),
+            out_specs=pl.BlockSpec(memory_space=pltpu.VMEM),
+            scratch_shapes=[
+                pltpu.VMEM((blocks, windows, channels, NS), jnp.bfloat16),
+                pltpu.VMEM((sources, 8, NS), jnp.float32),
+                pltpu.VMEM((windows, sources, LAG_ROWS, NS), jnp.bfloat16),
+                pltpu.VMEM((sources, LAG_ROWS, total // 2), jnp.bfloat16),
+                pltpu.VMEM((sources, LAG_ROWS, total // 2), jnp.bfloat16),
+                pltpu.SemaphoreType.DMA((4, blocks)),
+                pltpu.SemaphoreType.DMA((blocks,)),
+                pltpu.SemaphoreType.DMA,
+                pltpu.SemaphoreType.DMA,
+            ],
+            compiler_params=pltpu.CompilerParams(
+                vmem_limit_bytes=VMEM_LIMIT, collective_id=0, has_side_effects=True
+            ),
+            name="gather_correlate",
+        )(series)
     gathered = lax.all_gather(series, "chan", axis=0, tiled=False)
     place = jnp.stack([win_at, chan_at]).astype(jnp.int32)
-    scale = 1.0 / (math.sqrt(NS) * math.sqrt(windows * groups))
-    sources = channels // STRIDE
     scratch = [
         pltpu.VMEM((sources, 8, NS), jnp.float32),
         pltpu.VMEM((sources, LAG_ROWS, NS), jnp.bfloat16),
     ]
-    total = blocks * channels
-    if groups == 2:
-        own, other = pl.pallas_call(
-            lambda *refs: corr_pair_kernel(scale, *refs),
-            out_shape=[
-                jax.ShapeDtypeStruct((sources, LAGS, total // 2), jnp.float32),
-                jax.ShapeDtypeStruct((sources, LAG_ROWS, total // 2), jnp.bfloat16),
-            ],
-            in_specs=[smem] + whole_in_vmem(1),
-            out_specs=whole_in_vmem(2),
-            scratch_shapes=scratch,
-            compiler_params=params,
-            name="correlate",
-        )(place, gathered)
-        arrived = lax.ppermute(other, "win", [(0, 1), (1, 0)])
-        return own + arrived[:, :LAGS].astype(jnp.float32)
     own = pl.pallas_call(
         lambda *refs: corr_all_kernel(scale, *refs),
         out_shape=jax.ShapeDtypeStruct((sources, LAGS, total), jnp.float32),

time: 88.4 us -> 53 us (0.60)
  waiting for transfers between devices: 49.5 us -> 0 us
  Pallas kernels: 7.57 us -> 39.1 us
  between operations: 13.5 us -> 0.08 us
  local copies, waits for them, and re-layouts: 8.9 us -> 6.63 us
  starting transfers between devices: 1.54 us -> 0 us
    all_gather x1 -> x0, waiting for transfers between devices: 43.2 us -> none  [local(): gathered = lax.all_gather(series, 'chan', axis=0, tiled=False)]
    pallas_call x1, Pallas kernels: 4.14 us -> 36.3 us  [local(): pl.pallas_call(lambda *refs: gather_corr_kernel(scale, *refs), out_shape=...]
    ppermute x1 -> x0, waiting for transfers between devices: 6.29 us -> none  [local(): arrived = lax.ppermute(other, 'win', [(0, 1), (1, 0)])]
    unnamed x16 -> x14, local copies, waits for them, and re-layouts: 6.64 us -> 4.37 us
    ppermute x1 -> x0, starting transfers between devices: 1.54 us -> none  [local(): arrived = lax.ppermute(other, 'win', [(0, 1), (1, 0)])]
  transfers between devices with their start and end apart: 2 -> 0, of which waited for: 2 -> 0; matrix products, arithmetic and copies ran while one was open for 0% -> 0% of each run, Pallas kernels for 0% -> 0%
where the time goes in v2:
time: 53 us; the launch traced here: 52.7 us
  Pallas kernels  39.1 us (74%)
  local copies, waits for them, and re-layouts  6.63 us (13%)
  blocking collectives  6.17 us (12%)
  other arithmetic  0.75 us (1%)
    pallas_call x1, Pallas kernels, local(): pl.pallas_call(lambda *refs: gather_corr_kernel(scale, *refs), out_shape=...  36.3 us
    all_gather x1, blocking collectives, local(): record = lax.all_gather(strain_raw, 'win', axis=1, tiled=True)  6.17 us
    unnamed x14, local copies, waits for them, and re-layouts  4.37 us
    pallas_call x1, Pallas kernels, local(): pl.pallas_call(lambda *refs: whiten_kernel(windows, *refs), out_shape=jax...  2.77 us

profile of v2, /device:TPU:0, one launch (start us, length us, event | category | flops | bytes accessed | tf_op | source)
XLA Modules:
  0.0 52.7 jit_solution(8954417258324596795)
XLA Ops:
  0.0 0.0 copy-start
  0.0 0.7 %convert_bitcast_fusion = f32[16,1]{0,1:T(1,128)S(1)} fusion(s32[16]{0:T(128)} %param.12), kind=kLoop, calls=%fused_computation | loop fusion | flops 16 | bytes 128 | tf_op jit(solution)/shard_map/broadcast_in_dim | solution.py:344
  0.7 0.7 %concatenate.3 = bf16[644]{0:T(1024)(128)(2,1)S(1)} pad(bf16[128]{0:T(256)(128)(2,1)} %param.11, bf16[]{:T(256)} %constant.6.clone.1), padding=0_516 | pad | bytes 1546 | tf_op jit(solution)/shard_map/concatenate | solution.py:333
  1.4 0.1 copy.14.refs_9_
  1.5 6.2 %all_gather.3.refs_1_ = bf16[16,4352]{1,0:T(8,128)(2,1)S(1)} all-gather(bf16[16,2176]{1,0:T(8,128)(2,1)} %param.10), channel_id=1, replica_groups=mesh['win'=2,'chan'=16] {'win'}, dimensions={1}, use_global_device_ids=true | all-gather | bytes 208896 | tf_op jit(solution)/shard_map/all_gather | solution.py:332
  7.7 0.4 tile.10
  8.1 0.0 copy-start.4
  8.1 0.1 reshape.4
  8.2 0.0 copy-start.5
  8.2 0.2 copy.13
  8.4 0.0 copy-start.6
  8.4 0.0 copy-done
  8.4 0.7 %copy-done.4 = bf16[512,512]{1,0:T(8,128)(2,1)S(1)} copy-done((bf16[512,512]{1,0:T(8,128)(2,1)S(1)}, bf16[512,512]{1,0:T(8,128)(2,1)}, u32[]{:S(2)}) %copy-start.4) | copy-done | bytes 524312
  9.1 0.0 copy-done.5
  9.1 0.0 copy-done.6
  9.1 0.0 copy-start.1
  9.1 1.2 %copy-done.1 = bf16[2,512,512]{2,1,0:T(8,128)(2,1)S(1)} copy-done((bf16[2,512,512]{2,1,0:T(8,128)(2,1)S(1)}, bf16[2,512,512]{2,1,0:T(8,128)(2,1)}, u32[]{:S(2)}) %copy-start.1) | copy-done | bytes 1048600
  10.3 0.0 copy-start.2
  10.3 1.2 %copy-done.2 = bf16[2,512,512]{2,1,0:T(8,128)(2,1)S(1)} copy-done((bf16[2,512,512]{2,1,0:T(8,128)(2,1)S(1)}, bf16[2,512,512]{2,1,0:T(8,128)(2,1)}, u32[]{:S(2)}) %copy-start.2) | copy-done | bytes 1048600
  11.6 0.0 copy-start.3
  11.6 1.2 %copy-done.3 = bf16[2,512,512]{2,1,0:T(8,128)(2,1)S(1)} copy-done((bf16[2,512,512]{2,1,0:T(8,128)(2,1)S(1)}, bf16[2,512,512]{2,1,0:T(8,128)(2,1)}, u32[]{:S(2)}) %copy-start.3) | copy-done | bytes 1048600
  12.8 2.8 %whiten.1.refs_0_ = bf16[4,16,1024]{2,1,0:T(8,128)(2,1)S(1)} custom-call(s32[4]{0:T(128)S(1)} %copy-done.6, bf16[16,4352]{1,0:T(8,128)(2,1)S(1)} %all_gather.3.refs_1_, bf16[640,128]{1,0:T(8,128)(2,1)S(1)} %bitcast.3, bf16[2,512,512]{2,1,0:T(8,128)(2,1)S(1)} %copy-done.3, bf16[2,512,512]{2,1,0:T(8,128)(2,1)S(1)} %copy-done.2, ...), custom_call_target="tpu_custom_call" | custom-call | tf_op jit(solution)/shard_map/whiten/pallas_call | solution.py:337
  15.6 36.3 %gather_correlate.1 = f32[8,101,128]{2,1,0:T(8,128)S(1)} custom-call(bf16[4,16,1024]{2,1,0:T(8,128)(2,1)S(1)} %whiten.1.refs_0_), custom_call_target="tpu_custom_call" | custom-call | tf_op jit(solution)/shard_map/gather_correlate/pallas_call | solution.py:349
  51.9 0.8 %copy.15 = f32[8,101,128]{2,0,1:T(8,128)} copy(f32[8,101,128]{2,1,0:T(8,128)S(1)} %gather_correlate.1) | data formatting | bytes 827392 | tf_op jit(solution)/shard_map/gather_correlate/pallas_call | solution.py:349
  (2 shorter events, 0.0 us)
Async XLA Ops:
  0.0 8.4 %copy-start = (bf16[2,512,512]{2,1,0:T(8,128)(2,1)S(1)}, bf16[2,512,512]{2,1,0:T(8,128)(2,1)}, u32[]{:S(2)}) copy-start(bf16[2,512,512]{2,1,0:T(8,128)(2,1)} %constant.17.clone.refs_6_) | copy-start | bytes 3145732
  8.1 1.0 %copy-start.4 = (bf16[512,512]{1,0:T(8,128)(2,1)S(1)}, bf16[512,512]{1,0:T(8,128)(2,1)}, u32[]{:S(2)}) copy-start(bf16[512,512]{1,0:T(8,128)(2,1)} %constant.18.clone.refs_7_) | copy-start | bytes 1572868
  8.2 0.9 %copy-start.5 = (f32[8,512]{1,0:T(8,128)S(1)}, f32[8,512]{1,0:T(8,128)}, u32[]{:S(2)}) copy-start(f32[8,512]{1,0:T(8,128)} %constant.19.clone.refs_8_) | copy-start | bytes 49156
  8.4 0.7 %copy-start.6 = (s32[4]{0:T(128)S(1)}, s32[4]{0:T(128)}, u32[]{:S(2)}) copy-start(s32[4]{0:T(128)} %refs_0_.1) | copy-start | bytes 52
  9.1 1.2 %copy-start.1 = (bf16[2,512,512]{2,1,0:T(8,128)(2,1)S(1)}, bf16[2,512,512]{2,1,0:T(8,128)(2,1)}, u32[]{:S(2)}) copy-start(bf16[2,512,512]{2,1,0:T(8,128)(2,1)} %constant.16.clone.refs_5_) | copy-start | bytes 3145732
  10.3 1.2 %copy-start.2 = (bf16[2,512,512]{2,1,0:T(8,128)(2,1)S(1)}, bf16[2,512,512]{2,1,0:T(8,128)(2,1)}, u32[]{:S(2)}) copy-start(bf16[2,512,512]{2,1,0:T(8,128)(2,1)} %constant.15.clone.refs_4_) | copy-start | bytes 3145732
  11.6 1.2 %copy-start.3 = (bf16[2,512,512]{2,1,0:T(8,128)(2,1)S(1)}, bf16[2,512,512]{2,1,0:T(8,128)(2,1)}, u32[]{:S(2)}) copy-start(bf16[2,512,512]{2,1,0:T(8,128)(2,1)} %constant.14.clone.refs_3_) | copy-start | bytes 3145732

commit v3 on v2

--- a/solution.py
+++ b/solution.py
@@ -21,6 +21,7 @@
 BLOCK = 128
 REACH = BLOCK * DECIM + TAPS
 LAG_ROWS = 112
+CHUNKS = 2
 VMEM_LIMIT = 48 * 1024 * 1024
 
 
@@ -179,46 +180,49 @@
     held[me] = series[...]
     pl.semaphore_wait(barrier, 3 + has_above.astype(jnp.int32) + has_below.astype(jnp.int32))
 
-    def move(way, block, target):
+    chunk = windows // CHUNKS
+
+    def move(way, block, part, target):
+        span = held.at[block, pl.ds(part * chunk, chunk)]
         return pltpu.make_async_remote_copy(
-            src_ref=held.at[block],
-            dst_ref=held.at[block],
-            send_sem=sent.at[way, block],
-            recv_sem=landed.at[block],
+            src_ref=span,
+            dst_ref=span,
+            send_sem=sent.at[way, block, part],
+            recv_sem=landed.at[block, part],
             device_id=(win_at, target),
             device_id_type=mesh_id,
         )
 
-    def up(block):
-        return move(0, block, above)
-
-    def down(block):
-        return move(1, block, below)
-
-    def across(block):
-        return move(2, block, beside)
-
-    def over(block):
-        return move(3, block, twin)
-
-    def await_block(block):
-        move(2, block, beside).wait_recv()
+    def up(block, part):
+        return move(0, block, part, above)
+
+    def down(block, part):
+        return move(1, block, part, below)
+
+    def across(block, part):
+        return move(2, block, part, beside)
+
+    def over(block, part):
+        return move(3, block, part, twin)
+
+    def await_block(block, part):
+        across(block, part).wait_recv()
 
     def when(condition, action):
         @pl.when(condition)
         def _():
             action()
 
-    when(has_above, lambda: up(me).start())
-    when(has_below, lambda: down(me).start())
-    across(me).start()
-    over(me).start()
-
-    await_block(twin)
+    for part in range(CHUNKS):
+        when(has_above, lambda: up(me, part).start())
+        when(has_below, lambda: down(me, part).start())
+        across(me, part).start()
+        over(me, part).start()
+
     source_block = me // STRIDE * STRIDE
     source_part = lax.rem(me, STRIDE)
 
-    def build(window_at, carry):
+    def build(window_at):
         rows = held[source_block, window_at].astype(jnp.float32)
         chosen = jnp.where(source_part == 0, rows[:sources], rows[sources:])
         for row in range(8):
@@ -231,9 +235,9 @@
                 lagged[window_at, source, first : first + 16, :] = jnp.concatenate(pair, axis=0).astype(jnp.bfloat16)
             return carry
 
-        return lax.fori_loop(0, sources, build_source, carry)
-
-    def pass_lane(distance):
+        lax.fori_loop(0, sources, build_source, 0)
+
+    def pass_lane(distance, part):
         for sign in (-1, 1):
             origin = layer + sign * distance
             block = me + 4 * sign * distance
@@ -241,53 +245,67 @@
             further = has_above if sign < 0 else has_below
 
             def relay():
-                await_block(block)
-                when(further, lambda: (up if sign < 0 else down)(block).start())
-                across(block).start()
-                over(block).start()
+                await_block(block, part)
+                when(further, lambda: (up if sign < 0 else down)(block, part).start())
+                across(block, part).start()
+                over(block, part).start()
 
             when(exists, relay)
 
-    def pass_beside(distance):
+    def pass_beside(distance, part):
         for sign in (-1, 1) if distance else (1,):
             origin = layer + sign * distance
             block = origin * 4 + other_lane
             exists = (origin >= 0) if sign < 0 else (origin < layers)
 
             def relay():
-                await_block(block)
-                over(block).start()
+                await_block(block, part)
+                over(block, part).start()
 
             when(exists, relay)
 
-    lax.fori_loop(0, windows, build, 0)
-    pass_lane(1)
-    pass_beside(0)
-    for distance in range(2, layers):
-        pass_lane(distance)
-        pass_beside(distance - 1)
-    pass_beside(layers - 1)
-    for at in range(layers):
-        across_twin = at * 4 + lax.rem(twin_lane + 2, 4)
-        await_block(across_twin)
-        mine = at * 4 + twin_lane
-        when(mine != twin, lambda: await_block(mine))
-
+    to_build = list(range(windows))
+    for part in range(CHUNKS):
+        await_block(twin, part)
+    build(to_build.pop(0))
+    for distance in range(1, layers):
+        for part in range(CHUNKS):
+            pass_lane(distance, part)
+            if to_build:
+                build(to_build.pop(0))
+            pass_beside(distance - 1, part)
+    while to_build:
+        build(to_build.pop(0))
     half_blocks = blocks // 2
 
-    def half_sums(half):
+    def window_sums(half, window_at):
+        return lax.dot_general(
+            lagged[window_at].reshape(sources * LAG_ROWS, NS),
+            held[pl.ds(half * half_blocks, half_blocks), window_at].reshape(half_blocks * channels, NS),
+            (((1,), (1,)), ((), ())),
+            preferred_element_type=jnp.float32,
+        )
+
+    for part in range(CHUNKS):
+        pass_beside(layers - 1, part)
+    partial = None
+    for part in range(CHUNKS):
+        for at in range(layers):
+            await_block(at * 4 + lax.rem(twin_lane + 2, 4), part)
+            mine = at * 4 + twin_lane
+            when(mine != twin, lambda: await_block(mine, part))
+        for window_at in range(part * chunk, (part + 1) * chunk):
+            term = window_sums(partner, window_at)
+            partial = term if partial is None else partial + term
+
+    def own_sums():
         total = None
         for window_at in range(windows):
-            term = lax.dot_general(
-                lagged[window_at].reshape(sources * LAG_ROWS, NS),
-                held[pl.ds(half * half_blocks, half_blocks), window_at].reshape(half_blocks * channels, NS),
-                (((1,), (1,)), ((), ())),
-                preferred_element_type=jnp.float32,
-            )
+            term = window_sums(win_at, window_at)
             total = term if total is None else total + term
         return total * scale
 
-    outgoing[...] = half_sums(partner).astype(jnp.bfloat16).reshape(outgoing.shape)
+    outgoing[...] = (partial * scale).astype(jnp.bfloat16).reshape(outgoing.shape)
     swap = pltpu.make_async_remote_copy(
         src_ref=outgoing,
         dst_ref=arrived,
@@ -297,7 +315,7 @@
         device_id_type=mesh_id,
     )
     swap.start()
-    kept = half_sums(win_at).reshape(outgoing.shape)
+    kept = own_sums().reshape(outgoing.shape)
     swap.wait()
     total = kept + arrived[...].astype(jnp.float32)
     for source in range(sources):
@@ -305,11 +323,12 @@
 
     for at in range(layers):
         block = at * 4 + lane
-        when(jnp.logical_and(has_above, at <= layer), lambda: up(block).wait_send())
-        when(jnp.logical_and(has_below, at >= layer), lambda: down(block).wait_send())
-        across(block).wait_send()
-        over(block).wait_send()
-        over(at * 4 + other_lane).wait_send()
+        for part in range(CHUNKS):
+            when(jnp.logical_and(has_above, at <= layer), lambda: up(block, part).wait_send())
+            when(jnp.logical_and(has_below, at >= layer), lambda: down(block, part).wait_send())
+            across(block, part).wait_send()
+            over(block, part).wait_send()
+            over(at * 4 + other_lane, part).wait_send()
 
 
 def corr_all_kernel(scale, place, gathered, own, turned, lagged):
@@ -357,8 +376,8 @@
                 pltpu.VMEM((windows, sources, LAG_ROWS, NS), jnp.bfloat16),
                 pltpu.VMEM((sources, LAG_ROWS, total // 2), jnp.bfloat16),
                 pltpu.VMEM((sources, LAG_ROWS, total // 2), jnp.bfloat16),
-                pltpu.SemaphoreType.DMA((4, blocks)),
-                pltpu.SemaphoreType.DMA((blocks,)),
+                pltpu.SemaphoreType.DMA((4, blocks, CHUNKS)),
+                pltpu.SemaphoreType.DMA((blocks, CHUNKS)),
                 pltpu.SemaphoreType.DMA,
                 pltpu.SemaphoreType.DMA,
             ],

time: 53 us -> 48 us (0.906)
  Pallas kernels: 39.1 us -> 34.1 us
    pallas_call x1, Pallas kernels: 36.3 us -> 31.3 us  [local(): pl.pallas_call(lambda *refs: gather_corr_kernel(scale, *refs), out_shape=...]
where the time goes in v3:
time: 48 us; the launch traced here: 47.7 us
  Pallas kernels  34.1 us (71%)
  local copies, waits for them, and re-layouts  6.63 us (14%)
  blocking collectives  6.17 us (13%)
  other arithmetic  0.75 us (2%)
    pallas_call x1, Pallas kernels, local(): pl.pallas_call(lambda *refs: gather_corr_kernel(scale, *refs), out_shape=...  31.3 us
    all_gather x1, blocking collectives, local(): record = lax.all_gather(strain_raw, 'win', axis=1, tiled=True)  6.17 us
    unnamed x14, local copies, waits for them, and re-layouts  4.37 us
    pallas_call x1, Pallas kernels, local(): pl.pallas_call(lambda *refs: whiten_kernel(windows, *refs), out_shape=jax...  2.77 us

profile of v3, /device:TPU:0, one launch (start us, length us, event | category | flops | bytes accessed | tf_op | source)
XLA Modules:
  0.0 47.7 jit_solution(3515622640516890764)
XLA Ops:
  0.0 0.0 copy-start
  0.0 0.7 %convert_bitcast_fusion = f32[16,1]{0,1:T(1,128)S(1)} fusion(s32[16]{0:T(128)} %param.12), kind=kLoop, calls=%fused_computation | loop fusion | flops 16 | bytes 128 | tf_op jit(solution)/shard_map/broadcast_in_dim | solution.py:363
  0.7 0.7 %concatenate.3 = bf16[644]{0:T(1024)(128)(2,1)S(1)} pad(bf16[128]{0:T(256)(128)(2,1)} %param.11, bf16[]{:T(256)} %constant.6.clone.1), padding=0_516 | pad | bytes 1546 | tf_op jit(solution)/shard_map/concatenate | solution.py:352
  1.4 0.1 copy.14.refs_9_
  1.5 6.2 %all_gather.3.refs_1_ = bf16[16,4352]{1,0:T(8,128)(2,1)S(1)} all-gather(bf16[16,2176]{1,0:T(8,128)(2,1)} %param.10), channel_id=1, replica_groups=mesh['win'=2,'chan'=16] {'win'}, dimensions={1}, use_global_device_ids=true | all-gather | bytes 208896 | tf_op jit(solution)/shard_map/all_gather | solution.py:351
  7.7 0.4 tile.10
  8.1 0.0 copy-start.4
  8.1 0.1 reshape.4
  8.2 0.0 copy-start.5
  8.2 0.2 copy.13
  8.4 0.0 copy-start.6
  8.4 0.0 copy-done
  8.4 0.7 %copy-done.4 = bf16[512,512]{1,0:T(8,128)(2,1)S(1)} copy-done((bf16[512,512]{1,0:T(8,128)(2,1)S(1)}, bf16[512,512]{1,0:T(8,128)(2,1)}, u32[]{:S(2)}) %copy-start.4) | copy-done | bytes 524312
  9.1 0.0 copy-done.5
  9.1 0.0 copy-done.6
  9.1 0.0 copy-start.1
  9.1 1.2 %copy-done.1 = bf16[2,512,512]{2,1,0:T(8,128)(2,1)S(1)} copy-done((bf16[2,512,512]{2,1,0:T(8,128)(2,1)S(1)}, bf16[2,512,512]{2,1,0:T(8,128)(2,1)}, u32[]{:S(2)}) %copy-start.1) | copy-done | bytes 1048600
  10.3 0.0 copy-start.2
  10.3 1.2 %copy-done.2 = bf16[2,512,512]{2,1,0:T(8,128)(2,1)S(1)} copy-done((bf16[2,512,512]{2,1,0:T(8,128)(2,1)S(1)}, bf16[2,512,512]{2,1,0:T(8,128)(2,1)}, u32[]{:S(2)}) %copy-start.2) | copy-done | bytes 1048600
  11.6 0.0 copy-start.3
  11.6 1.2 %copy-done.3 = bf16[2,512,512]{2,1,0:T(8,128)(2,1)S(1)} copy-done((bf16[2,512,512]{2,1,0:T(8,128)(2,1)S(1)}, bf16[2,512,512]{2,1,0:T(8,128)(2,1)}, u32[]{:S(2)}) %copy-start.3) | copy-done | bytes 1048600
  12.8 2.8 %whiten.1.refs_0_ = bf16[4,16,1024]{2,1,0:T(8,128)(2,1)S(1)} custom-call(s32[4]{0:T(128)S(1)} %copy-done.6, bf16[16,4352]{1,0:T(8,128)(2,1)S(1)} %all_gather.3.refs_1_, bf16[640,128]{1,0:T(8,128)(2,1)S(1)} %bitcast.3, bf16[2,512,512]{2,1,0:T(8,128)(2,1)S(1)} %copy-done.3, bf16[2,512,512]{2,1,0:T(8,128)(2,1)S(1)} %copy-done.2, ...), custom_call_target="tpu_custom_call" | custom-call | tf_op jit(solution)/shard_map/whiten/pallas_call | solution.py:356
  15.6 31.3 %gather_correlate.1 = f32[8,101,128]{2,1,0:T(8,128)S(1)} custom-call(bf16[4,16,1024]{2,1,0:T(8,128)(2,1)S(1)} %whiten.1.refs_0_), custom_call_target="tpu_custom_call" | custom-call | tf_op jit(solution)/shard_map/gather_correlate/pallas_call | solution.py:368
  46.9 0.8 %copy.15 = f32[8,101,128]{2,0,1:T(8,128)} copy(f32[8,101,128]{2,1,0:T(8,128)S(1)} %gather_correlate.1) | data formatting | bytes 827392 | tf_op jit(solution)/shard_map/gather_correlate/pallas_call | solution.py:368
  (2 shorter events, 0.0 us)
Async XLA Ops:
  0.0 8.4 %copy-start = (bf16[2,512,512]{2,1,0:T(8,128)(2,1)S(1)}, bf16[2,512,512]{2,1,0:T(8,128)(2,1)}, u32[]{:S(2)}) copy-start(bf16[2,512,512]{2,1,0:T(8,128)(2,1)} %constant.17.clone.refs_6_) | copy-start | bytes 3145732
  8.1 1.0 %copy-start.4 = (bf16[512,512]{1,0:T(8,128)(2,1)S(1)}, bf16[512,512]{1,0:T(8,128)(2,1)}, u32[]{:S(2)}) copy-start(bf16[512,512]{1,0:T(8,128)(2,1)} %constant.18.clone.refs_7_) | copy-start | bytes 1572868
  8.2 0.9 %copy-start.5 = (f32[8,512]{1,0:T(8,128)S(1)}, f32[8,512]{1,0:T(8,128)}, u32[]{:S(2)}) copy-start(f32[8,512]{1,0:T(8,128)} %constant.19.clone.refs_8_) | copy-start | bytes 49156
  8.4 0.7 %copy-start.6 = (s32[4]{0:T(128)S(1)}, s32[4]{0:T(128)}, u32[]{:S(2)}) copy-start(s32[4]{0:T(128)} %refs_0_.1) | copy-start | bytes 52
  9.1 1.2 %copy-start.1 = (bf16[2,512,512]{2,1,0:T(8,128)(2,1)S(1)}, bf16[2,512,512]{2,1,0:T(8,128)(2,1)}, u32[]{:S(2)}) copy-start(bf16[2,512,512]{2,1,0:T(8,128)(2,1)} %constant.16.clone.refs_5_) | copy-start | bytes 3145732
  10.3 1.2 %copy-start.2 = (bf16[2,512,512]{2,1,0:T(8,128)(2,1)S(1)}, bf16[2,512,512]{2,1,0:T(8,128)(2,1)}, u32[]{:S(2)}) copy-start(bf16[2,512,512]{2,1,0:T(8,128)(2,1)} %constant.15.clone.refs_4_) | copy-start | bytes 3145732
  11.6 1.2 %copy-start.3 = (bf16[2,512,512]{2,1,0:T(8,128)(2,1)S(1)}, bf16[2,512,512]{2,1,0:T(8,128)(2,1)}, u32[]{:S(2)}) copy-start(bf16[2,512,512]{2,1,0:T(8,128)(2,1)} %constant.14.clone.refs_3_) | copy-start | bytes 3145732

commit v4 on v3

--- a/solution.py
+++ b/solution.py
@@ -22,7 +22,7 @@
 REACH = BLOCK * DECIM + TAPS
 LAG_ROWS = 112
 CHUNKS = 2
-VMEM_LIMIT = 48 * 1024 * 1024
+VMEM_LIMIT = 60 * 1024 * 1024
 
 
 def split_table(table):
@@ -77,20 +77,84 @@
     return both[:rows] + both[rows:] + dot(value_high, low)
 
 
-def whiten_kernel(windows, starts, record, band, forward_high, forward_low, inverse_high, inverse_low,
-                  mean_table, edge, live, out):
-    channels, length = record.shape
+def start_tables(sources, places, arrivals):
+    copies = [pltpu.make_async_copy(source, place, arrivals.at[at])
+              for at, (source, place) in enumerate(zip(sources, places))]
+    for copy in copies:
+        copy.start()
+    return copies
+
+
+def band_rows(taps):
+    rows = jnp.concatenate([taps, jnp.zeros((1, REACH - TAPS), jnp.float32)], axis=1)
+    rows = jnp.broadcast_to(rows, (BLOCK, REACH))
+    row_at = lax.broadcasted_iota(jnp.int32, (BLOCK, REACH), 0)
+    step = 1
+    while step < BLOCK:
+        rows = jnp.where(row_at // step % 2 == 1, pltpu.roll(rows, step * DECIM, 1), rows)
+        step *= 2
+    return rows.astype(jnp.bfloat16)
+
+
+def whiten_pair_kernel(windows, starts, live, strain, taps, *refs):
+    sources, out, record = refs[:6], refs[6], refs[7]
+    places, (arrivals, sent, landed) = refs[8:14], refs[14:]
+    copies = start_tables(sources, places, arrivals)
+    win_at = lax.axis_index("win")
+    partner = (1 - win_at, lax.axis_index("chan"))
+    barrier = pltpu.get_barrier_semaphore()
+    pl.semaphore_signal(barrier, inc=1, device_id=partner, device_id_type=pl.DeviceIdType.MESH)
+    pl.semaphore_wait(barrier, 1)
+    swap = pltpu.make_async_remote_copy(
+        src_ref=strain,
+        dst_ref=record.at[win_at],
+        send_sem=sent,
+        recv_sem=landed,
+        device_id=partner,
+        device_id_type=pl.DeviceIdType.MESH,
+    )
+    swap.start()
+    record[win_at] = strain[...]
+    band = band_rows(taps[...])
+    swap.wait()
+    wide = jnp.concatenate([record[0].astype(jnp.float32), record[1].astype(jnp.float32)], axis=1)
+    for copy in copies:
+        copy.wait()
+    whiten_rows(windows, starts, live, wide, band, places, out)
+
+
+def whiten_all_kernel(windows, starts, live, record, taps, *refs):
+    sources, out, places, arrivals = refs[:6], refs[6], refs[7:13], refs[13]
+    copies = start_tables(sources, places, arrivals)
+    band = band_rows(taps[...])
     wide = record[...].astype(jnp.float32)
+    for copy in copies:
+        copy.wait()
+    whiten_rows(windows, starts, live, wide, band, places, out)
+
+
+def whiten_rows(windows, starts, live, wide, band, places, out):
+    forward_high, forward_low, inverse_high, inverse_low, mean_table, edge = places
+    channels, length = wide.shape
     pieces = []
     for window_at in range(windows):
         start = starts[window_at]
         rolled = pltpu.roll(wide, lax.rem(length - start, length), 1).astype(jnp.bfloat16)
         parts = [
-            dot(rolled[:, at * BLOCK * DECIM : at * BLOCK * DECIM + REACH], band[...])
+            lax.dot_general(
+                rolled[:, at * BLOCK * DECIM : at * BLOCK * DECIM + REACH],
+                band,
+                (((1,), (1,)), ((), ())),
+                preferred_element_type=jnp.float32,
+            )
             for at in range(NS // BLOCK)
         ]
         pieces.append(jnp.concatenate(parts, axis=1))
     decimated = jnp.concatenate(pieces, axis=0)
+    row_at = lax.broadcasted_iota(jnp.int32, (channels, NS), 0)
+    kept = jnp.zeros((channels, NS), jnp.float32)
+    for channel in range(channels):
+        kept = jnp.where(row_at == channel, live[channel].astype(jnp.float32), kept)
     first, second = decimated[:, :FOLD], decimated[:, FOLD:]
     even = split_dot(first + second, forward_high[0], forward_low[0])
     odd = split_dot(first - second, forward_high[1], forward_low[1])
@@ -116,7 +180,7 @@
     series = jnp.concatenate([from_even + from_odd, from_even - from_odd], axis=1)
     for window_at in range(windows):
         rows = series[window_at * channels : (window_at + 1) * channels]
-        out[window_at] = (rows * live[...]).astype(jnp.bfloat16)
+        out[window_at] = (rows * kept).astype(jnp.bfloat16)
 
 
 def lag_sums(place, gathered, turned, lagged):
@@ -348,19 +412,35 @@
     blocks = lax.axis_size("chan")
     win_at = lax.axis_index("win")
     chan_at = lax.axis_index("chan")
-    record = lax.all_gather(strain_raw, "win", axis=1, tiled=True)
-    padded = jnp.concatenate([fir_taps, jnp.zeros((REACH + DECIM - TAPS,), fir_taps.dtype)])
-    band = jnp.tile(padded, BLOCK)[: BLOCK * REACH].reshape(BLOCK, REACH).T
     params = pltpu.CompilerParams(vmem_limit_bytes=VMEM_LIMIT)
     smem = pl.BlockSpec(memory_space=pltpu.SMEM)
-    series = pl.pallas_call(
-        lambda *refs: whiten_kernel(windows, *refs),
+    places = [pltpu.VMEM(table.shape, table.dtype) for table in tables]
+    taps = fir_taps.astype(jnp.float32)[None, :]
+    whiten_specs = dict(
         out_shape=jax.ShapeDtypeStruct((windows, channels, NS), jnp.bfloat16),
-        in_specs=[smem] + whole_in_vmem(9),
+        in_specs=[smem, smem] + whole_in_vmem(2) + [pl.BlockSpec(memory_space=pltpu.HBM)] * len(tables),
         out_specs=pl.BlockSpec(memory_space=pltpu.VMEM),
-        compiler_params=params,
         name="whiten",
-    )(window_start, record, band, *tables, live_mask.astype(jnp.float32)[:, None])
+    )
+    if groups == 2:
+        series = pl.pallas_call(
+            lambda *refs: whiten_pair_kernel(windows, *refs),
+            scratch_shapes=[pltpu.VMEM((2,) + strain_raw.shape, strain_raw.dtype)]
+            + places
+            + [pltpu.SemaphoreType.DMA((len(tables),)), pltpu.SemaphoreType.DMA, pltpu.SemaphoreType.DMA],
+            compiler_params=pltpu.CompilerParams(
+                vmem_limit_bytes=VMEM_LIMIT, collective_id=1, has_side_effects=True
+            ),
+            **whiten_specs,
+        )(window_start, live_mask, strain_raw, taps, *tables)
+    else:
+        record = lax.all_gather(strain_raw, "win", axis=1, tiled=True)
+        series = pl.pallas_call(
+            lambda *refs: whiten_all_kernel(windows, *refs),
+            scratch_shapes=places + [pltpu.SemaphoreType.DMA((len(tables),))],
+            compiler_params=params,
+            **whiten_specs,
+        )(window_start, live_mask, record, taps, *tables)
     scale = 1.0 / (math.sqrt(NS) * math.sqrt(windows * groups))
     sources = channels // STRIDE
     total = blocks * channels

time: 48 us -> 46.1 us (0.960)
  Pallas kernels: 34.1 us -> 42.9 us
  blocking collectives: 6.17 us -> 0 us
  local copies, waits for them, and re-layouts: 6.63 us -> 1.84 us
    pallas_call x1, Pallas kernels: 2.77 us -> 9.87 us  [local(): pl.pallas_call(lambda *refs: whiten_pair_kernel(windows, *refs), scratch_...]
    all_gather x1 -> x0, blocking collectives: 6.17 us -> none  [local(): record = lax.all_gather(strain_raw, 'win', axis=1, tiled=True)]
    unnamed x14 -> x0, local copies, waits for them, and re-layouts: 4.37 us -> none
    pallas_call x1, Pallas kernels: 31.3 us -> 33 us  [local(): pl.pallas_call(lambda *refs: gather_corr_kernel(scale, *refs), out_shape=...]
    pallas_call x1, local copies, waits for them, and re-layouts: 0.83 us -> 1.84 us  [local(): pl.pallas_call(lambda *refs: gather_corr_kernel(scale, *refs), out_shape=...]
    concatenate x1 -> x0, local copies, waits for them, and re-layouts: 0.66 us -> none  [local(): jnp.concatenate([fir_taps, jnp.zeros((REACH + DECIM - TAPS,), fir_taps.dt...]
where the time goes in v4:
time: 46.1 us; the launch traced here: 45.9 us
  Pallas kernels  42.9 us (93%)
  local copies, waits for them, and re-layouts  1.84 us (4%)
  other arithmetic  1.17 us (3%)
    pallas_call x1, Pallas kernels, local(): pl.pallas_call(lambda *refs: gather_corr_kernel(scale, *refs), out_shape=...  33 us
    pallas_call x1, Pallas kernels, local(): pl.pallas_call(lambda *refs: whiten_pair_kernel(windows, *refs), scratch_...  9.87 us
    pallas_call x1, local copies, waits for them, and re-layouts, local(): pl.pallas_call(lambda *refs: gather_corr_kernel(scale, *refs), out_shape=...  1.84 us
    broadcast_in_dim x1, other arithmetic, local(): taps = fir_taps.astype(jnp.float32)[None, :]  1.17 us

profile of v4, /device:TPU:0, one launch (start us, length us, event | category | flops | bytes accessed | tf_op | source)
XLA Modules:
  0.0 45.9 jit_solution(1557226888721482830)
XLA Ops:
  0.0 1.2 %bitcast_convert_fusion.refs_3_ = f32[1,128]{1,0:T(1,128)} fusion(bf16[128]{0:T(256)(128)(2,1)} %param.11), kind=kLoop, calls=%fused_computation | loop fusion | flops 128 | bytes 768 | tf_op jit(solution)/shard_map/broadcast_in_dim | solution.py:418
  1.2 9.9 %whiten.1.refs_0_ = bf16[4,16,1024]{2,1,0:T(8,128)(2,1)} custom-call(s32[4]{0:T(128)} %refs_0_.1, s32[16]{0:T(128)} %refs_1_.1, bf16[16,2176]{1,0:T(8,128)(2,1)} %refs_2_.1, f32[1,128]{1,0:T(1,128)} %bitcast_convert_fusion.refs_3_, bf16[2,512,512]{2,1,0:T(8,128)(2,1)} %constant.12.clone.refs_4_, bf16[2,512,512]{2,1,0:T(8,128)(2,1)} %constant.13.clone.refs_5_, ...), custom_call_target="tpu_custom_call" | custom-call | tf_op jit(solution)/shard_map/whiten/pallas_call | solution.py:426
  11.1 33.0 %gather_correlate.1 = f32[8,101,128]{2,1,0:T(8,128)} custom-call(bf16[4,16,1024]{2,1,0:T(8,128)(2,1)} %whiten.1.refs_0_), custom_call_target="tpu_custom_call" | custom-call | tf_op jit(solution)/shard_map/gather_correlate/pallas_call | solution.py:448
  44.1 1.8 %copy.11 = f32[8,101,128]{2,0,1:T(8,128)} copy(f32[8,101,128]{2,1,0:T(8,128)} %gather_correlate.1) | data formatting | bytes 827392 | tf_op jit(solution)/shard_map/gather_correlate/pallas_call | solution.py:448

commit v5 on v4

--- a/solution.py
+++ b/solution.py
@@ -23,6 +23,7 @@
 LAG_ROWS = 112
 CHUNKS = 2
 VMEM_LIMIT = 60 * 1024 * 1024
+CORR_VMEM_LIMIT = 40 * 1024 * 1024
 
 
 def split_table(table):
@@ -462,7 +463,7 @@
                 pltpu.SemaphoreType.DMA,
             ],
             compiler_params=pltpu.CompilerParams(
-                vmem_limit_bytes=VMEM_LIMIT, collective_id=0, has_side_effects=True
+                vmem_limit_bytes=CORR_VMEM_LIMIT, collective_id=0, has_side_effects=True
             ),
             name="gather_correlate",
         )(series)

time: 46.1 us -> 44.3 us (0.961)
  Pallas kernels: 42.9 us -> 41.2 us
    pallas_call x1, Pallas kernels: 33 us -> 31.3 us  [local(): pl.pallas_call(lambda *refs: gather_corr_kernel(scale, *refs), out_shape=...]
    pallas_call x1, local copies, waits for them, and re-layouts: 1.84 us -> 0.83 us  [local(): pl.pallas_call(lambda *refs: gather_corr_kernel(scale, *refs), out_shape=...]
    unnamed x0 -> x2, local copies, waits for them, and re-layouts: none -> 0.9 us
where the time goes in v5:
time: 44.3 us; the launch traced here: 44.1 us
  Pallas kernels  41.2 us (93%)
  local copies, waits for them, and re-layouts  1.73 us (4%)
  other arithmetic  1.17 us (3%)
    pallas_call x1, Pallas kernels, local(): pl.pallas_call(lambda *refs: gather_corr_kernel(scale, *refs), out_shape=...  31.3 us
    pallas_call x1, Pallas kernels, local(): pl.pallas_call(lambda *refs: whiten_pair_kernel(windows, *refs), scratch_...  9.89 us
    broadcast_in_dim x1, other arithmetic, local(): taps = fir_taps.astype(jnp.float32)[None, :]  1.17 us
    unnamed x2, local copies, waits for them, and re-layouts  0.9 us

profile of v5, /device:TPU:0, one launch (start us, length us, event | category | flops | bytes accessed | tf_op | source)
XLA Modules:
  0.0 44.1 jit_solution(13484024516742502641)
XLA Ops:
  0.0 1.2 %bitcast_convert_fusion.refs_3_ = f32[1,128]{1,0:T(1,128)} fusion(bf16[128]{0:T(256)(128)(2,1)} %param.11), kind=kLoop, calls=%fused_computation | loop fusion | flops 128 | bytes 768 | tf_op jit(solution)/shard_map/broadcast_in_dim | solution.py:419
  1.2 9.9 %whiten.1.refs_0_ = bf16[4,16,1024]{2,1,0:T(8,128)(2,1)} custom-call(s32[4]{0:T(128)} %refs_0_.1, s32[16]{0:T(128)} %refs_1_.1, bf16[16,2176]{1,0:T(8,128)(2,1)} %refs_2_.1, f32[1,128]{1,0:T(1,128)} %bitcast_convert_fusion.refs_3_, bf16[2,512,512]{2,1,0:T(8,128)(2,1)} %constant.12.clone.refs_4_, bf16[2,512,512]{2,1,0:T(8,128)(2,1)} %constant.13.clone.refs_5_, ...), custom_call_target="tpu_custom_call" | custom-call | tf_op jit(solution)/shard_map/whiten/pallas_call | solution.py:427
  11.1 0.0 copy-start
  11.1 0.9 %copy-done = bf16[4,16,1024]{2,1,0:T(8,128)(2,1)S(1)} copy-done((bf16[4,16,1024]{2,1,0:T(8,128)(2,1)S(1)}, bf16[4,16,1024]{2,1,0:T(8,128)(2,1)}, u32[]{:S(2)}) %copy-start) | copy-done | bytes 131096
  12.0 31.3 %gather_correlate.1 = f32[8,101,128]{2,1,0:T(8,128)S(1)} custom-call(bf16[4,16,1024]{2,1,0:T(8,128)(2,1)S(1)} %copy-done), custom_call_target="tpu_custom_call" | custom-call | tf_op jit(solution)/shard_map/gather_correlate/pallas_call | solution.py:449
  43.3 0.8 %copy.11 = f32[8,101,128]{2,0,1:T(8,128)} copy(f32[8,101,128]{2,1,0:T(8,128)S(1)} %gather_correlate.1) | data formatting | bytes 827392 | tf_op jit(solution)/shard_map/gather_correlate/pallas_call | solution.py:449
Async XLA Ops:
  11.1 0.9 %copy-start = (bf16[4,16,1024]{2,1,0:T(8,128)(2,1)S(1)}, bf16[4,16,1024]{2,1,0:T(8,128)(2,1)}, u32[]{:S(2)}) copy-start(bf16[4,16,1024]{2,1,0:T(8,128)(2,1)} %whiten.1.refs_0_) | copy-start | bytes 393220

commit v6 on v5

--- a/solution.py
+++ b/solution.py
@@ -21,7 +21,7 @@
 BLOCK = 128
 REACH = BLOCK * DECIM + TAPS
 LAG_ROWS = 112
-CHUNKS = 2
+CHUNKS = 4
 VMEM_LIMIT = 60 * 1024 * 1024
 CORR_VMEM_LIMIT = 40 * 1024 * 1024
 

time: 44.3 us -> 46.1 us (1.041)
  Pallas kernels: 41.2 us -> 43 us
    pallas_call x1, Pallas kernels: 31.3 us -> 33.1 us  [local(): pl.pallas_call(lambda *refs: gather_corr_kernel(scale, *refs), out_shape=...]
where the time goes in v6:
time: 46.1 us; the launch traced here: 45.9 us
  Pallas kernels  43 us (93%)
  local copies, waits for them, and re-layouts  1.73 us (4%)
  other arithmetic  1.17 us (3%)
    pallas_call x1, Pallas kernels, local(): pl.pallas_call(lambda *refs: gather_corr_kernel(scale, *refs), out_shape=...  33.1 us
    pallas_call x1, Pallas kernels, local(): pl.pallas_call(lambda *refs: whiten_pair_kernel(windows, *refs), scratch_...  9.89 us
    broadcast_in_dim x1, other arithmetic, local(): taps = fir_taps.astype(jnp.float32)[None, :]  1.17 us

profile of v6, /device:TPU:0, one launch (start us, length us, event | category | flops | bytes accessed | tf_op | source)
XLA Modules:
  0.0 45.9 jit_solution(1753763290061830053)
XLA Ops:
  0.0 1.2 %bitcast_convert_fusion.refs_3_ = f32[1,128]{1,0:T(1,128)} fusion(bf16[128]{0:T(256)(128)(2,1)} %param.11), kind=kLoop, calls=%fused_computation | loop fusion | flops 128 | bytes 768 | tf_op jit(solution)/shard_map/broadcast_in_dim | solution.py:419
  1.2 9.9 %whiten.1.refs_0_ = bf16[4,16,1024]{2,1,0:T(8,128)(2,1)} custom-call(s32[4]{0:T(128)} %refs_0_.1, s32[16]{0:T(128)} %refs_1_.1, bf16[16,2176]{1,0:T(8,128)(2,1)} %refs_2_.1, f32[1,128]{1,0:T(1,128)} %bitcast_convert_fusion.refs_3_, bf16[2,512,512]{2,1,0:T(8,128)(2,1)} %constant.12.clone.refs_4_, bf16[2,512,512]{2,1,0:T(8,128)(2,1)} %constant.13.clone.refs_5_, ...), custom_call_target="tpu_custom_call" | custom-call | tf_op jit(solution)/shard_map/whiten/pallas_call | solution.py:427
  11.1 0.0 copy-start
  11.1 0.9 %copy-done = bf16[4,16,1024]{2,1,0:T(8,128)(2,1)S(1)} copy-done((bf16[4,16,1024]{2,1,0:T(8,128)(2,1)S(1)}, bf16[4,16,1024]{2,1,0:T(8,128)(2,1)}, u32[]{:S(2)}) %copy-start) | copy-done | bytes 131096
  12.0 33.1 %gather_correlate.1 = f32[8,101,128]{2,1,0:T(8,128)S(1)} custom-call(bf16[4,16,1024]{2,1,0:T(8,128)(2,1)S(1)} %copy-done), custom_call_target="tpu_custom_call" | custom-call | tf_op jit(solution)/shard_map/gather_correlate/pallas_call | solution.py:449
  45.1 0.8 %copy.11 = f32[8,101,128]{2,0,1:T(8,128)} copy(f32[8,101,128]{2,1,0:T(8,128)S(1)} %gather_correlate.1) | data formatting | bytes 827392 | tf_op jit(solution)/shard_map/gather_correlate/pallas_call | solution.py:449
Async XLA Ops:
  11.1 0.9 %copy-start = (bf16[4,16,1024]{2,1,0:T(8,128)(2,1)S(1)}, bf16[4,16,1024]{2,1,0:T(8,128)(2,1)}, u32[]{:S(2)}) copy-start(bf16[4,16,1024]{2,1,0:T(8,128)(2,1)} %whiten.1.refs_0_) | copy-start | bytes 393220
